TPU v7x, 128 devices: a whole 4x4x4 slice. The times are simulated.
128 devices in a mesh: dp: 4 (over y_lo, core), fsdp: 32 (over x, z, y_hi).
Axes of the slice: x: 4, y: 4 (y_hi: 2, y_lo: 2; y = y_hi * 2 + y_lo), z: 4, core: 2. Of those that a mesh axis runs over, the one named last changes fastest.
Arguments:
- normed: bfloat16 [65536, 8192], P(('dp', 'fsdp')), may hold values from -24 to 24
- queries: bfloat16 [65536, 4096], P(('dp', 'fsdp')), may hold values from -96 to 96, as said below
- keys: bfloat16 [65536, 512], P(('dp', 'fsdp')), may hold values from -4.5 to 4.5
- value_weight: bfloat16 [8192, 512], P('fsdp'), may hold values from -0.0625 to 0.0625
- iterate: float32 [8192, 512], P('fsdp'), may hold values from -6 to 6
- residual: float32 [8192, 512], P('fsdp'), may hold values from -6 to 6
- direction: float32 [8192, 512], P('fsdp'), may hold values from -6 to 6
- damping: float32 [1], replicated, may hold values from 0.05 to 0.5
Outputs:
- new_iterate: float32 [8192, 512], P('fsdp')
- new_residual: float32 [8192, 512], P('fsdp')
- new_direction: float32 [8192, 512], P('fsdp')
Inputs may be any that keep to these rules, and one draw needn't show every extreme that they name: `queries`: queries are of order one except for a few rows, which may be large multiples of an earlier key of their key-value head.
All inputs are finite; a program needn't handle non-finite values.
Results may differ from a plain program's by a relative error of at most 0.0043.
Values may be sent and summed in bfloat16 or wider, within the bound.
No kernel may reach another device: no remote copies, remote signals or barrier semaphores. Data moves between devices by JAX's collectives and lax.ppermute only.
A program may use at most 192 MiB of HBM per device.

v0:
```python
import math
import jax
import jax.numpy as jnp
from jax import lax
from jax.sharding import PartitionSpec as P

HD = 128
EPSILON = 1e-05


def group_pull(query_rows, key_rows, value_rows, tangent_rows, head_size):
    seq_len = query_rows.shape[0]
    per_group = query_rows.shape[1] // head_size
    queries_split = query_rows.reshape(seq_len, per_group, head_size)
    scores = jnp.einsum(
        "tjd,sd->jts", queries_split, key_rows, preferred_element_type=jnp.float32
    ) / math.sqrt(head_size)
    positions = lax.iota(jnp.int32, seq_len)
    causal = positions[:, None] >= positions[None, :]
    scores = jnp.where(causal, scores, -jnp.inf)
    highest = jnp.max(scores, axis=-1, keepdims=True)
    exps = jnp.exp(scores - highest)
    weights_soft = (exps / jnp.sum(exps, axis=-1, keepdims=True)).astype(jnp.bfloat16)
    outputs = jnp.einsum(
        "jts,sd->tjd", weights_soft, value_rows, preferred_element_type=jnp.float32
    )
    tangents = jnp.einsum(
        "jts,sd->tjd", weights_soft, tangent_rows, preferred_element_type=jnp.float32
    )
    inverse = lax.rsqrt(jnp.mean(outputs * outputs, axis=-1, keepdims=True) + EPSILON)
    normal_out = outputs * inverse

    def jacobian(vector):
        return (
            vector - normal_out * jnp.mean(normal_out * vector, axis=-1, keepdims=True)
        ) * inverse

    wback = jacobian(jacobian(tangents)).astype(jnp.bfloat16)
    return jnp.einsum(
        "jts,tjd->sd", weights_soft, wback, preferred_element_type=jnp.float32
    ).astype(jnp.bfloat16)


def body(normed, queries, keys, value_weight, iterate, residual, direction, damping):
    seq_len = normed.shape[0]
    kv_width = keys.shape[1]
    kv_heads = kv_width // HD
    per_group = queries.shape[1] // kv_width
    dir_half = direction.astype(jnp.bfloat16)
    columns = normed
    projected = jnp.dot(
        columns,
        lax.all_gather(value_weight, "fsdp", axis=0, tiled=True),
        preferred_element_type=jnp.float32,
    )
    tangent = jnp.dot(
        columns,
        lax.all_gather(dir_half, "fsdp", axis=0, tiled=True),
        preferred_element_type=jnp.float32,
    )
    projected = projected.astype(jnp.bfloat16)
    tangent = tangent.astype(jnp.bfloat16)
    pulled_parts = []
    for group_index in range(kv_heads):
        query_cols = queries[:, group_index * per_group * HD : (group_index + 1) * per_group * HD]
        lower = group_index * HD
        pulled_parts.append(
            group_pull(
                query_cols,
                keys[:, lower : lower + HD],
                projected[:, lower : lower + HD],
                tangent[:, lower : lower + HD],
                HD,
            )
        )
    pulled = jnp.concatenate(pulled_parts, axis=1)
    tokens_all = lax.axis_size("dp") * lax.axis_size("fsdp") * seq_len
    columns = normed
    shard_sum = lax.psum_scatter(
        jnp.dot(columns.T, pulled, preferred_element_type=jnp.float32),
        "fsdp",
        scatter_dimension=0,
        tiled=True,
    )
    summed = lax.psum(shard_sum, "dp")
    hessian_dir = summed / tokens_all + damping[0] * direction
    old_sq = lax.psum(jnp.sum(residual * residual), "fsdp")
    curv_sum = lax.psum(jnp.sum(direction * hessian_dir), "fsdp")
    step_size = old_sq / curv_sum
    new_iterate = iterate + step_size * direction
    new_residual = residual - step_size * hessian_dir
    new_sq = lax.psum(jnp.sum(new_residual * new_residual), "fsdp")
    new_direction = new_residual + new_sq / old_sq * direction
    return (new_iterate, new_residual, new_direction)


def solution(mesh):
    return jax.shard_map(
        body,
        mesh=mesh,
        in_specs=(
            P(("dp", "fsdp"), None),
            P(("dp", "fsdp"), None),
            P(("dp", "fsdp"), None),
            P("fsdp", None),
            P("fsdp", None),
            P("fsdp", None),
            P("fsdp", None),
            P(),
        ),
        out_specs=(P("fsdp", None), P("fsdp", None), P("fsdp", None)),
        check_vma=False,
    )
```

profile of v0, /device:TPU:16, one launch (start us, length us, event | category | flops | bytes accessed | tf_op | source)
XLA Modules:
  0.0 863.5 jit_solution(4124391215796967002)
XLA Ops:
  7.9 1.8 convert_element_type.46
  9.8 3.9 fusion.124
  13.7 2.3 copy.97
  16.0 1.4 copy.99
  18.5 7.2 fusion.125
  25.7 7.2 fusion.135
  33.0 7.2 fusion.130
  40.2 7.1 fusion.140
  47.3 7.2 divide_convert_fusion
  54.5 3.5 divide_convert_fusion.2
  58.3 3.4 divide_convert_fusion.1
  61.7 0.9 slice-done.5
  62.6 3.3 divide_convert_fusion.3
  65.9 49.1 %all-gather.5.cloned.1.call-done = bf16[8192,512]{1,0:T(8,128)(2,1)} async-done(((bf16[256,512]{1,0:T(8,128)(2,1)}), bf16[8192,512]{1,0:T(8,128)(2,1)}) %all-gather.5.cloned.1.call-update) | async-done | bytes 8388624 | tf_op jit(solution)/shard_map/all_gather | solution.py:53
  115.0 10.4 %convolution_convert_fusion = bf16[512,512]{1,0:T(8,128)(2,1)S(1)} fusion(bf16[512,8192]{1,0:T(8,128)(2,1)} %param.8, bf16[8192,512]{1,0:T(8,128)(2,1)} %all-gather.5.cloned.1.call-done), kind=kOutput, calls=%fused_computation.69 | convolution fusion | flops 4295229440 | bytes 17301504 | tf_op jit(solution)/shard_map/dot_general | solution.py:51
  126.2 94.4 %all-gather.3.cloned.1.call-done = bf16[8192,512]{1,0:T(8,128)(2,1)} async-done(((bf16[256,512]{1,0:T(8,128)(2,1)}), bf16[8192,512]{1,0:T(8,128)(2,1)}) %all-gather.3.cloned.1.call-update) | async-done | bytes 8388624 | tf_op jit(solution)/shard_map/all_gather | solution.py:58
  220.6 10.4 %convolution_convert_fusion.1 = bf16[512,512]{1,0:T(8,128)(2,1)S(1)} fusion(bf16[512,8192]{1,0:T(8,128)(2,1)} %param.8, bf16[8192,512]{1,0:T(8,128)(2,1)} %all-gather.3.cloned.1.call-done), kind=kOutput, calls=%fused_computation.70 | convolution fusion | flops 4295229440 | bytes 17301504 | tf_op jit(solution)/shard_map/dot_general | solution.py:56
  232.4 1.5 fusion.35
  236.8 1.3 fusion.33
  238.1 0.9 copy-done.1
  241.1 1.3 fusion.34
  245.5 1.3 fusion.32
  246.9 0.9 slice-done.1
  247.8 8.2 convolution_bitcast_fusion
  256.0 360.2 %reduce-scatter.2.cloned.1.call-done = f32[256,512]{0,1:T(8,128)} async-done(((f32[8192,512]{0,1:T(8,128)}), f32[256,512]{0,1:T(8,128)}) %reduce-scatter.2.cloned.1.call-update) | async-done | bytes 524304 | tf_op jit(solution)/shard_map/reduce_scatter | solution.py:79
  618.1 43.0 %all-reduce.3.cloned.1.call-done = f32[256,512]{0,1:T(8,128)} async-done(((f32[256,512]{0,1:T(8,128)}), f32[256,512]{0,1:T(8,128)}) %all-reduce.3.cloned.1.call-update) | async-done | bytes 524304 | tf_op jit(solution)/shard_map/psum | solution.py:85
  661.0 1.9 multiply_reduce_fusion.5
  663.1 90.6 %all-reduce = (f32[]{:T(128)}, f32[]{:T(128)}) all-reduce(f32[]{:T(128)} %multiply_reduce_fusion.6, f32[]{:T(128)} %multiply_reduce_fusion.5), channel_id=1, replica_groups=mesh['dp'=4,'fsdp'=32] {'fsdp'}, use_global_device_ids=true, to_apply=%region_1.2 | all-reduce | flops 2 | bytes 16 | tf_op jit(solution)/shard_map/psum | solution.py:87
  755.8 96.4 %psum.31 = f32[]{:T(128)} all-reduce(f32[]{:T(128)} %get-tuple-element.11), channel_id=1, replica_groups=mesh['dp'=4,'fsdp'=32] {'fsdp'}, use_global_device_ids=true, to_apply=%region_27.28 | all-reduce | flops 1 | bytes 8 | tf_op jit(solution)/shard_map/psum | solution.py:92
  853.5 1.0 copy.67
  854.6 1.0 copy.68
  855.6 1.0 copy.66
  (77 shorter events, 14.6 us)
Async XLA Ops:
  7.2 107.8 %all-gather.5.cloned.1.call-start = ((), (), s32[]{:S(2)}) async-start(), calls=%async_computation.2 | async-start | bytes 8650752 | tf_op jit(solution)/shard_map/all_gather | solution.py:53
  7.9 212.7 %all-gather.3.cloned.1.call-start = ((), (), s32[]{:S(2)}) async-start(), calls=%async_computation.1 | async-start | bytes 8650752 | tf_op jit(solution)/shard_map/all_gather | solution.py:58
  9.7 606.5 %reduce-scatter.2.cloned.1.call-start = ((), (), s32[]{:S(2)}) async-start(), calls=%async_computation.3 | async-start | bytes 17301504 | tf_op jit(solution)/shard_map/reduce_scatter | solution.py:79
  25.7 7.2 copy-start.10
  32.9 7.2 copy-start.9
  47.3 7.2 copy-start.5
  47.3 10.6 %slice-start.2 = ((s8[8388608]{0:T(1024)(128)(4,1)}), s8[4194304]{0:T(1024)(128)(4,1)S(1)}, s32[]{:S(2)}) async-start(s8[8388608]{0:T(1024)(128)(4,1)} %bitcast.284), calls=%async_computation.7 | async-start | bytes 8388608
  54.5 3.8 slice-start.3
  54.5 7.2 slice-start.4
  58.3 4.3 slice-start.5
  115.0 10.4 %copy-start.3 = (bf16[8,512,512]{1,2,0:T(8,128)(2,1)S(1)}, bf16[8,512,512]{1,2,0:T(8,128)(2,1)}, u32[]{:S(2)}) copy-start(bf16[8,512,512]{1,2,0:T(8,128)(2,1)} %divide_convert_fusion) | copy-start | bytes 12582916
  220.6 10.4 %copy-start.4 = (bf16[8,512,512]{1,2,0:T(8,128)(2,1)S(1)}, bf16[8,512,512]{1,2,0:T(8,128)(2,1)}, u32[]{:S(2)}) copy-start(bf16[8,512,512]{1,2,0:T(8,128)(2,1)} %divide_convert_fusion) | copy-start | bytes 12582916
  232.4 2.2 copy-start.2
  236.8 2.2 copy-start.1
  241.1 2.2 copy-start
  244.1 2.8 slice-start
  244.9 2.9 slice-start.1
  255.9 360.3 %copy-start.6 = (f32[256,512]{1,0:T(8,128)S(1)}, f32[256,512]{1,0:T(8,128)}, u32[]{:S(2)}) copy-start(f32[256,512]{1,0:T(8,128)} %param.14) | copy-start | bytes 1572868
  255.9 361.2 %copy-start.7 = (f32[256,512]{1,0:T(8,128)S(1)}, f32[256,512]{1,0:T(8,128)}, u32[]{:S(2)}) copy-start(f32[256,512]{1,0:T(8,128)} %param.13) | copy-start | bytes 1572868
  256.0 405.1 %all-reduce.3.cloned.1.call-start = ((), (), s32[]{:S(2)}) async-start(), calls=%async_computation.4 | async-start | bytes 1048576 | tf_op jit(solution)/shard_map/psum | solution.py:85
  616.2 46.7 %copy-start.11 = (f32[256,512]{1,0:T(8,128)S(1)}, f32[256,512]{1,0:T(8,128)}, u32[]{:S(2)}) copy-start(f32[256,512]{1,0:T(8,128)} %param.12) | copy-start | bytes 1572868
  661.0 94.0 %copy-start.8 = (f32[256,512]{0,1:T(8,128)S(1)}, f32[256,512]{0,1:T(8,128)}, u32[]{:S(2)}) copy-start(f32[256,512]{0,1:T(8,128)} %all-reduce.3.cloned.1.call-done) | copy-start | bytes 1572868
Sparse Core Ops, SparseCore 0:
  11.0 103.9 all-gather.4
  118.6 101.9 all-gather.2
  256.1 360.0 reduce-scatter.1
  618.6 42.4 all-reduce.2
where the time goes:
time: 874 us; the launch traced here: 864 us
  waiting for transfers between devices  547 us (63%)
  blocking collectives  187 us (21%)
  matrix products  69.3 us (8%)
  other arithmetic  25 us (3%)
  between operations  17.9 us (2%)
  local copies, waits for them, and re-layouts  16.8 us (2%)
    reduce_scatter x1, waiting for transfers between devices, body(): lax.psum_scatter(jnp.dot(columns.T, pulled, preferred_element_type=jnp.fl...  360 us
    psum x1, blocking collectives, body(): new_sq = lax.psum(jnp.sum(new_residual * new_residual), 'fsdp')  96.4 us
    all_gather x1, waiting for transfers between devices, body(): lax.all_gather(dir_half, 'fsdp', axis=0, tiled=True)  94.4 us
    psum x1, blocking collectives, body(): old_sq = lax.psum(jnp.sum(residual * residual), 'fsdp')  90.6 us
    all_gather x1, waiting for transfers between devices, body(): lax.all_gather(value_weight, 'fsdp', axis=0, tiled=True)  49.1 us
    psum x1, waiting for transfers between devices, body(): summed = lax.psum(shard_sum, 'dp')  43 us
    sub x4, matrix products, group_pull(): exps = jnp.exp(scores - highest)  28.8 us
  transfers between devices with their start and end apart: 4, of which 4 were waited for; matrix products, arithmetic and copies ran while one was open for 8% of the time, Pallas kernels for 0%

commit v1 on v0

--- a/solution.py
+++ b/solution.py
@@ -3,9 +3,17 @@
 import jax.numpy as jnp
 from jax import lax
 from jax.sharding import PartitionSpec as P
+from jax.lax import all_to_all, axis_size
 
 HD = 128
 EPSILON = 1e-05
+
+
+def sheet_finish(mine_x, array_axis):
+    known = jnp.concatenate(
+        all_to_all(jnp.stack([mine_x] * axis_size("fsdp")), "fsdp", 0, 0), array_axis
+    )
+    return known
 
 
 def group_pull(query_rows, key_rows, value_rows, tangent_rows, head_size):
@@ -53,11 +61,7 @@
         lax.all_gather(value_weight, "fsdp", axis=0, tiled=True),
         preferred_element_type=jnp.float32,
     )
-    tangent = jnp.dot(
-        columns,
-        lax.all_gather(dir_half, "fsdp", axis=0, tiled=True),
-        preferred_element_type=jnp.float32,
-    )
+    tangent = jnp.dot(columns, sheet_finish(dir_half, 0), preferred_element_type=jnp.float32)
     projected = projected.astype(jnp.bfloat16)
     tangent = tangent.astype(jnp.bfloat16)
     pulled_parts = []

time: 874 us -> 863 us (0.987)
  waiting for transfers between devices: 547 us -> 529 us
  starting transfers between devices: 0.16 us -> 11.1 us
    all_gather x1 -> x0, waiting for transfers between devices: 94.4 us -> none  [body(): lax.all_gather(dir_half, 'fsdp', axis=0, tiled=True)]
    all_to_all x0 -> x1, waiting for transfers between devices: none -> 77.2 us  [sheet_finish(): all_to_all(jnp.stack([mine_x] * axis_size('fsdp')), 'fsdp', 0, 0)]
    all_to_all x0 -> x1, starting transfers between devices: none -> 10.9 us  [sheet_finish(): all_to_all(jnp.stack([mine_x] * axis_size('fsdp')), 'fsdp', 0, 0)]
where the time goes in v1:
time: 863 us; the launch traced here: 859 us
  waiting for transfers between devices  529 us (61%)
  blocking collectives  187 us (22%)
  matrix products  69.4 us (8%)
  other arithmetic  24.3 us (3%)
  local copies, waits for them, and re-layouts  21.3 us (2%)
  between operations  17.7 us (2%)
  starting transfers between devices  11.1 us (1%)
    reduce_scatter x1, waiting for transfers between devices, body(): lax.psum_scatter(jnp.dot(columns.T, pulled, preferred_element_type=jnp.fl...  360 us
    psum x1, blocking collectives, body(): new_sq = lax.psum(jnp.sum(new_residual * new_residual), 'fsdp')  96.4 us
    psum x1, blocking collectives, body(): old_sq = lax.psum(jnp.sum(residual * residual), 'fsdp')  90.6 us
    all_to_all x1, waiting for transfers between devices, sheet_finish(): all_to_all(jnp.stack([mine_x] * axis_size('fsdp')), 'fsdp', 0, 0)  77.2 us
    all_gather x1, waiting for transfers between devices, body(): lax.all_gather(value_weight, 'fsdp', axis=0, tiled=True)  47.3 us
    psum x1, waiting for transfers between devices, body(): summed = lax.psum(shard_sum, 'dp')  43.2 us
    sub x4, matrix products, group_pull(): exps = jnp.exp(scores - highest)  29.1 us
    convert_element_type x4, other arithmetic, group_pull(): (exps / jnp.sum(exps, axis=-1, keepdims=True)).astype(jnp.bfloat16)  17.3 us
  transfers between devices with their start and end apart: 4, of which 4 were waited for; matrix products, arithmetic and copies ran while one was open for 8% of the time, Pallas kernels for 0%

profile of v1, /device:TPU:16, one launch (start us, length us, event | category | flops | bytes accessed | tf_op | source)
XLA Modules:
  0.0 859.4 jit_solution(11687842627330032611)
XLA Ops:
  7.9 1.1 convert_element_type.46
  9.0 4.2 stack.2
  13.1 10.9 %all-to-all-start = ((bf16[32,256,512]{2,1,0:T(8,128)(2,1)}), bf16[32,256,512]{2,1,0:T(8,128)(2,1)}, u32[]{:S(2)}, u32[]{:S(2)}) async-start(bf16[32,256,512]{2,1,0:T(8,128)(2,1)} %stack.2), calls=%async_computation | async-start | bytes 16777216 | tf_op jit(solution)/shard_map/all_to_all | solution.py:14
  24.2 3.9 fusion.124
  28.1 2.3 copy.97
  30.4 1.3 copy.98
  32.3 1.0 copy.100
  33.4 7.6 fusion.140
  41.0 7.1 fusion.135
  48.2 7.1 fusion.130
  55.3 7.2 fusion.125
  62.5 7.1 divide_convert_fusion.3
  69.6 3.5 divide_convert_fusion.2
  73.1 3.5 divide_convert_fusion.1
  76.5 1.1 slice-done.5
  77.6 3.3 divide_convert_fusion
  80.9 77.2 %all-to-all-done = bf16[32,256,512]{2,1,0:T(8,128)(2,1)} async-done(((bf16[32,256,512]{2,1,0:T(8,128)(2,1)}), bf16[32,256,512]{2,1,0:T(8,128)(2,1)}, u32[]{:S(2)}, u32[]{:S(2)}) %all-to-all-start) | async-done | bytes 8388640 | tf_op jit(solution)/shard_map/all_to_all | solution.py:14
  158.1 10.2 %convolution_convert_fusion.1 = bf16[512,512]{1,0:T(8,128)(2,1)S(1)} fusion(bf16[512,8192]{1,0:T(8,128)(2,1)} %param.8, bf16[8192,512]{1,0:T(8,128)(2,1)} %bitcast.3), kind=kOutput, calls=%fused_computation.70 | convolution fusion | flops 4295229440 | bytes 17301504 | tf_op jit(solution)/shard_map/dot_general | solution.py:64
  168.3 47.3 %all-gather.2.cloned.1.call-done = bf16[8192,512]{1,0:T(8,128)(2,1)} async-done(((bf16[256,512]{1,0:T(8,128)(2,1)}), bf16[8192,512]{1,0:T(8,128)(2,1)}) %all-gather.2.cloned.1.call-update) | async-done | bytes 8388624 | tf_op jit(solution)/shard_map/all_gather | solution.py:61
  215.6 10.4 %convolution_convert_fusion = bf16[512,512]{1,0:T(8,128)(2,1)S(1)} fusion(bf16[512,8192]{1,0:T(8,128)(2,1)} %param.8, bf16[8192,512]{1,0:T(8,128)(2,1)} %all-gather.2.cloned.1.call-done), kind=kOutput, calls=%fused_computation.69 | convolution fusion | flops 4295229440 | bytes 17301504 | tf_op jit(solution)/shard_map/dot_general | solution.py:59
  228.2 1.5 fusion.32
  232.6 1.3 fusion.33
  237.0 1.3 fusion.34
  241.4 1.3 fusion.35
  243.6 8.2 convolution_bitcast_fusion
  251.9 360.2 %reduce-scatter.2.cloned.1.call-done = f32[256,512]{0,1:T(8,128)} async-done(((f32[8192,512]{0,1:T(8,128)}), f32[256,512]{0,1:T(8,128)}) %reduce-scatter.2.cloned.1.call-update) | async-done | bytes 524304 | tf_op jit(solution)/shard_map/reduce_scatter | solution.py:83
  613.9 43.2 %all-reduce.3.cloned.1.call-done = f32[256,512]{0,1:T(8,128)} async-done(((f32[256,512]{0,1:T(8,128)}), f32[256,512]{0,1:T(8,128)}) %all-reduce.3.cloned.1.call-update) | async-done | bytes 524304 | tf_op jit(solution)/shard_map/psum | solution.py:89
  657.1 1.9 multiply_reduce_fusion.5
  659.2 90.6 %all-reduce = (f32[]{:T(128)}, f32[]{:T(128)}) all-reduce(f32[]{:T(128)} %multiply_reduce_fusion.6, f32[]{:T(128)} %multiply_reduce_fusion.5), channel_id=1, replica_groups=mesh['dp'=4,'fsdp'=32] {'fsdp'}, use_global_device_ids=true, to_apply=%region_1.2 | all-reduce | flops 2 | bytes 16 | tf_op jit(solution)/shard_map/psum | solution.py:91
  751.8 96.4 %psum.31 = f32[]{:T(128)} all-reduce(f32[]{:T(128)} %get-tuple-element.11), channel_id=1, replica_groups=mesh['dp'=4,'fsdp'=32] {'fsdp'}, use_global_device_ids=true, to_apply=%region_27.28 | all-reduce | flops 1 | bytes 8 | tf_op jit(solution)/shard_map/psum | solution.py:96
  849.6 1.0 copy.67
  850.7 1.0 copy.66
  (73 shorter events, 16.5 us)
Async XLA Ops:
  7.2 208.5 %all-gather.2.cloned.1.call-start = ((), (), s32[]{:S(2)}) async-start(), calls=%async_computation.2 | async-start | bytes 8650752 | tf_op jit(solution)/shard_map/all_gather | solution.py:61
  13.1 145.0 %all-to-all-start = ((bf16[32,256,512]{2,1,0:T(8,128)(2,1)}), bf16[32,256,512]{2,1,0:T(8,128)(2,1)}, u32[]{:S(2)}, u32[]{:S(2)}) async-start(bf16[32,256,512]{2,1,0:T(8,128)(2,1)} %stack.2), calls=%async_computation | async-start | bytes 16777216 | tf_op jit(solution)/shard_map/all_to_all | solution.py:14
  24.1 588.0 %reduce-scatter.2.cloned.1.call-start = ((), (), s32[]{:S(2)}) async-start(), calls=%async_computation.3 | async-start | bytes 17301504 | tf_op jit(solution)/shard_map/reduce_scatter | solution.py:83
  33.4 7.6 copy-start.8
  62.5 7.1 copy-start.4
  62.5 10.6 %slice-start.2 = ((s8[8388608]{0:T(1024)(128)(4,1)}), s8[4194304]{0:T(1024)(128)(4,1)S(1)}, s32[]{:S(2)}) async-start(s8[8388608]{0:T(1024)(128)(4,1)} %bitcast.285), calls=%async_computation.7 | async-start | bytes 8388608
  69.6 3.5 slice-start.3
  69.6 6.9 slice-start.4
  73.1 4.5 slice-start.5
  215.6 10.4 %copy-start.3 = (bf16[8,512,512]{1,2,0:T(8,128)(2,1)S(1)}, bf16[8,512,512]{1,2,0:T(8,128)(2,1)}, u32[]{:S(2)}) copy-start(bf16[8,512,512]{1,2,0:T(8,128)(2,1)} %divide_convert_fusion.3) | copy-start | bytes 12582916
  228.2 2.2 copy-start.2
  232.6 2.2 copy-start.1
  237.0 2.2 copy-start
  239.9 2.8 slice-start
  240.8 2.9 slice-start.1
  251.8 360.3 %copy-start.5 = (f32[256,512]{1,0:T(8,128)S(1)}, f32[256,512]{1,0:T(8,128)}, u32[]{:S(2)}) copy-start(f32[256,512]{1,0:T(8,128)} %param.14) | copy-start | bytes 1572868
  251.8 361.2 %copy-start.6 = (f32[256,512]{1,0:T(8,128)S(1)}, f32[256,512]{1,0:T(8,128)}, u32[]{:S(2)}) copy-start(f32[256,512]{1,0:T(8,128)} %param.13) | copy-start | bytes 1572868
  251.8 405.3 %all-reduce.3.cloned.1.call-start = ((), (), s32[]{:S(2)}) async-start(), calls=%async_computation.4 | async-start | bytes 1048576 | tf_op jit(solution)/shard_map/psum | solution.py:89
  612.1 46.9 %copy-start.9 = (f32[256,512]{1,0:T(8,128)S(1)}, f32[256,512]{1,0:T(8,128)}, u32[]{:S(2)}) copy-start(f32[256,512]{1,0:T(8,128)} %param.12) | copy-start | bytes 1572868
  657.1 94.0 %copy-start.7 = (f32[256,512]{0,1:T(8,128)S(1)}, f32[256,512]{0,1:T(8,128)}, u32[]{:S(2)}) copy-start(f32[256,512]{0,1:T(8,128)} %all-reduce.3.cloned.1.call-done) | copy-start | bytes 1572868
Sparse Core Ops, SparseCore 0:
  11.0 204.5 all-gather.1
  251.9 360.0 reduce-scatter.1
  614.6 42.4 all-reduce.2
